TPU v7x, 256 devices: a whole 4x4x8 slice. The times are simulated.
256 devices in a mesh: rep: 16 (over y, z_lo), row: 16 (over x, z_hi, core).
Axes of the slice: x: 4, y: 4, z: 8 (z_hi: 2, z_lo: 4; z = z_hi * 4 + z_lo), core: 2. Of those that a mesh axis runs over, the one named last changes fastest.
Arguments:
- features: bfloat16 [16, 6144, 256], P('rep', 'row'), may hold values from -6 to 6
- weight: bfloat16 [256, 256], replicated, may hold values from -0.375 to 0.375
- block_cols: int32 [16, 768, 3], P('rep', 'row'), may hold values from 0 to 47
- edge_counts: int32 [16, 768, 3, 128, 128], P('rep', 'row'), may hold values from 0 to 5
- cotangent: bfloat16 [16, 6144, 256], P('row', 'rep'), may hold values from -6 to 6
Outputs:
- activated: bfloat16 [16, 6144, 256], P('row', 'rep')
- grad_features: bfloat16 [16, 6144, 256], P('rep', 'row')
- grad_weight: float32 [256, 256], replicated
Inputs may be any that keep to these rules, and one draw needn't show every extreme that they name: `block_cols`: a block row may name the same column tile more than once.
All inputs are finite; a program needn't handle non-finite values.
Results may differ from a plain program's by a relative error of at most 0.0063.
Values may be sent and summed in bfloat16 or wider, within the bound.
A program may use at most 128 MiB of HBM per device.

v0:
```python
import jax
import jax.numpy as jnp
from jax import lax
from jax.sharding import PartitionSpec as P


def shards(features, weight, block_cols, edge_counts, cotangent):
    tile_size = edge_counts.shape[-1]
    feat_width = features.shape[-1]
    columns = block_cols[0]
    counts = edge_counts[0].astype(jnp.bfloat16)
    gathered = lax.all_gather(features[0], "row", axis=0, tiled=True)
    feat_tiles = gathered.reshape(-1, tile_size, feat_width)
    col_tiles = feat_tiles.shape[0]
    picked = feat_tiles[columns]
    partial_value = jnp.einsum(
        "rkij,rkjf->rif", counts, picked, preferred_element_type=jnp.float32
    ).reshape(-1, feat_width)
    rowsum = jnp.sum(edge_counts[0], axis=(1, 3)).astype(jnp.float32).reshape(-1)
    raw_sum, degree_sum = (
        lax.psum_scatter(partial_value, "rep", scatter_dimension=0, tiled=True),
        lax.psum_scatter(rowsum, "rep", scatter_dimension=0, tiled=True),
    )
    row_scale = lax.rsqrt(1.0 + degree_sum)
    summed = raw_sum * row_scale[:, None]
    aggregated = summed.astype(jnp.bfloat16)
    grad_rows = cotangent[0]
    preact = jnp.dot(aggregated, weight, preferred_element_type=jnp.float32)
    gate_value = jax.nn.sigmoid(preact)
    activated = (preact * gate_value).astype(jnp.bfloat16)
    grad_pre = (
        grad_rows.astype(jnp.float32) * gate_value * (1.0 + preact * (1.0 - gate_value))
    ).astype(jnp.bfloat16)
    back_proj = lax.dot_general(
        grad_pre, weight, (((1,), (1,)), ((), ())), preferred_element_type=jnp.float32
    )
    scaled_grad = (back_proj * row_scale[:, None]).astype(jnp.bfloat16)
    slab_grad = lax.all_gather(scaled_grad, "rep", axis=0, tiled=True)
    weight_part = lax.dot_general(
        aggregated, grad_pre, (((0,), (0,)), ((), ())), preferred_element_type=jnp.float32
    )
    grad_weight = lax.psum(weight_part, ("rep", "row"))
    grad_tiles = slab_grad.reshape(-1, tile_size, feat_width)
    contrib = jnp.einsum("rkij,rif->rkjf", counts, grad_tiles, preferred_element_type=jnp.float32)
    col_sum = jax.ops.segment_sum(
        contrib.reshape(-1, tile_size, feat_width), columns.reshape(-1), num_segments=col_tiles
    )
    grad_cols = lax.psum_scatter(
        col_sum.reshape(-1, feat_width), "row", scatter_dimension=0, tiled=True
    )
    return (activated[None], grad_cols.astype(jnp.bfloat16)[None], grad_weight)


def solution(mesh):
    placed = (
        P("rep", "row", None),
        P(),
        P("rep", "row", None),
        P("rep", "row", None, None, None),
        P("row", "rep", None),
    )
    return jax.shard_map(
        shards,
        mesh=mesh,
        in_specs=placed,
        out_specs=(P("row", "rep", None), P("rep", "row", None), P()),
        check_vma=False,
    )
```

profile of v0, /device:TPU:1, one launch (start us, length us, event | category | flops | bytes accessed | tf_op | source)
XLA Modules:
  0.0 795.3 jit_solution(16375944814481851645)
XLA Ops:
  7.2 0.0 copy-start
  7.2 0.0 all-gather.6.cloned.1.call-start
  7.2 0.7 all-gather.6.cloned.1.call-update
  7.9 0.0 reduce-scatter.3.cloned.1.call-start
  8.0 0.7 compare_select_fusion
  8.6 0.1 copy.13
  8.7 0.1 reshape.64
  8.9 76.3 %all-gather.6.cloned.1.call-done = bf16[1,6144,256]{2,1,0:T(8,128)(2,1)} async-done(((bf16[1,384,256]{2,1,0:T(8,128)(2,1)}), bf16[1,6144,256]{2,1,0:T(8,128)(2,1)}) %all-gather.6.cloned.1.call-update) | async-done | bytes 3145744 | tf_op jit(solution)/shard_map/all_gather | solution.py:12
  85.2 9.1 %gather_fusion = bf16[144,128,256]{2,1,0:T(8,128)(2,1)} fusion(bf16[48,128,256]{2,1,0:T(8,128)(2,1)} %bitcast.45, s32[1024]{0:T(1024)S(1)} %pad_clamp_fusion), kind=kCustom, calls=%fused_computation | custom fusion | bytes 18874944 | tf_op jit(solution)/shard_map/gather | solution.py:15
  94.3 10.9 %fusion.2 = f32[48,256,128,1]{1,2,3,0:T(8,128)} fusion(bf16[48,3,128,256]{3,2,1,0:T(8,128)(2,1)} %bitcast.44, s32[1,48,3,128,128]{4,3,2,1,0:T(8,128)} %param.8), kind=kOutput, calls=%fused_computation.4 | convolution fusion | flops 1210318848 | bytes 25165824 | tf_op jit(solution)/shard_map/rkij,rkjf->rif/dot_general | solution.py:16
  105.2 0.0 copy-start.5
  105.2 0.0 copy-start.4
  105.2 0.0 copy-start.3
  105.2 0.0 reduce-scatter.3.cloned.1.call-update
  105.2 0.0 all-gather.4.cloned.1.call-start
  105.3 4.6 reduce_sum.9
  109.9 0.0 copy-done.5
  109.9 0.6 dynamic-slice
  111.1 71.9 %all-reduce = f32[6144]{0:T(1024)S(1)} all-reduce(f32[6144]{0:T(1024)S(1)} %convert_bitcast_fusion.1), channel_id=4, replica_groups=mesh['rep'=16,'row'=16] {'rep'}, use_global_device_ids=true, to_apply=%region_2.0.clone | all-reduce | flops 6144 | bytes 49152
  183.1 0.1 fusion.10
  183.1 63.9 %reduce-scatter.3.cloned.1.call-done = f32[384,256]{1,0:T(8,128)} async-done(((f32[6144,256]{1,0:T(8,128)}), f32[384,256]{1,0:T(8,128)}) %reduce-scatter.3.cloned.1.call-update) | async-done | bytes 393232 | tf_op jit(solution)/shard_map/reduce_scatter | solution.py:21
  247.0 0.0 copy-done
  247.0 0.0 copy-done.4
  247.0 2.1 fusion.8
  249.1 0.9 fusion.6
  250.0 0.0 all-gather.4.cloned.1.call-update
  250.0 0.0 reduce-scatter.5.cloned.1.call-start
  250.1 0.0 copy-done.3
  250.1 0.1 copy.14
  250.2 0.1 reshape.72
  250.3 81.5 %all-gather.4.cloned.1.call-done = bf16[6144,256]{1,0:T(8,128)(2,1)} async-done(((bf16[384,256]{1,0:T(8,128)(2,1)}), bf16[6144,256]{1,0:T(8,128)(2,1)}) %all-gather.4.cloned.1.call-update) | async-done | bytes 3145744 | tf_op jit(solution)/shard_map/all_gather | solution.py:38
  331.9 13.8 %fusion = f32[48,256,3,128]{3,1,2,0:T(8,128)} fusion(bf16[48,128,256,1]{2,1,3,0:T(8,128)(2,1)} %bitcast.47, s32[1,48,3,128,128]{4,3,2,1,0:T(8,128)} %param.8), kind=kOutput, calls=%fused_computation.2 | convolution fusion | flops 1210318848 | bytes 31457280 | tf_op jit(solution)/shard_map/rkij,rif->rkjf/dot_general | solution.py:44
  345.6 18.6 %copy.16 = f32[144,128,256]{2,1,0:T(8,128)} copy(f32[144,128,256]{1,2,0:T(8,128)} %bitcast.43) | data formatting | bytes 37748736 | tf_op jit(solution)/shard_map/reshape | solution.py:46
  364.2 3.3 broadcast_in_dim.13
  367.6 0.0 copy-start.2
  367.6 0.0 copy-start.1
  367.6 41.9 %scatter_fusion = f32[48,128,256]{2,1,0:T(8,128)} fusion(f32[48,128,256]{2,1,0:T(8,128)} %broadcast_in_dim.13, s32[144]{0:T(256)S(1)} %reshape.72, f32[144,128,256]{2,1,0:T(8,128)} %copy.16), kind=kCustom, calls=%fused_computation.1 | custom fusion | flops 4718592 | bytes 56623680 | tf_op jit(solution)/shard_map/scatter-add | solution.py:45
  409.5 0.0 reduce-scatter.5.cloned.1.call-update
  409.5 0.0 all-reduce.3.cloned.1.call-start
  409.5 0.0 copy-done.2
  409.5 1.1 fusion.11
  410.6 0.0 all-reduce.3.cloned.1.call-update
  410.6 124.5 %reduce-scatter.5.cloned.1.call-done = f32[384,256]{1,0:T(8,128)} async-done(((f32[6144,256]{1,0:T(8,128)}), f32[384,256]{1,0:T(8,128)}) %reduce-scatter.5.cloned.1.call-update) | async-done | bytes 393232 | tf_op jit(solution)/shard_map/reduce_scatter | solution.py:48
  535.1 1.7 convert_bitcast_fusion
  536.8 250.3 %all-reduce.3.cloned.1.call-done = f32[256,256]{1,0:T(8,128)} async-done(((f32[256,256]{1,0:T(8,128)}), f32[256,256]{1,0:T(8,128)}) %all-reduce.3.cloned.1.call-update) | async-done | bytes 262160 | tf_op jit(solution)/shard_map/psum | solution.py:42
  787.1 1.7 copy.23
  788.8 0.0 copy-done.1
  (2 shorter events, 0.0 us)
Async XLA Ops:
  7.2 239.8 %copy-start = (bf16[256,256]{1,0:T(8,128)(2,1)S(1)}, bf16[256,256]{1,0:T(8,128)(2,1)}, u32[]{:S(2)}) copy-start(bf16[256,256]{1,0:T(8,128)(2,1)} %param.6) | copy-start | bytes 393220
  7.2 78.0 %all-gather.6.cloned.1.call-start = ((), (), s32[]{:S(2)}) async-start(), calls=%async_computation.6 | async-start | bytes 3342336 | tf_op jit(solution)/shard_map/all_gather | solution.py:12
  7.9 239.1 %reduce-scatter.3.cloned.1.call-start = ((), (), s32[]{:S(2)}) async-start(), calls=%async_computation.2 | async-start | bytes 6684672 | tf_op jit(solution)/shard_map/reduce_scatter | solution.py:21
  105.2 4.7 copy-start.5
  105.2 141.8 %copy-start.4 = (bf16[1,384,256]{2,1,0:T(8,128)(2,1)S(1)}, bf16[1,384,256]{2,1,0:T(8,128)(2,1)}, u32[]{:S(2)}) copy-start(bf16[1,384,256]{2,1,0:T(8,128)(2,1)} %param.9) | copy-start | bytes 589828
  105.2 144.9 %copy-start.3 = (s32[1,48,3]{1,0,2:T(1,128)S(1)}, s32[1,48,3]{1,0,2:T(1,128)}, u32[]{:S(2)}) copy-start(s32[1,48,3]{1,0,2:T(1,128)} %param.7) | copy-start | bytes 1732
  105.2 226.7 %all-gather.4.cloned.1.call-start = ((), (), s32[]{:S(2)}) async-start(), calls=%async_computation.3 | async-start | bytes 3342336 | tf_op jit(solution)/shard_map/all_gather | solution.py:38
  250.0 285.0 %reduce-scatter.5.cloned.1.call-start = ((), (), s32[]{:S(2)}) async-start(), calls=%async_computation.4 | async-start | bytes 6684672 | tf_op jit(solution)/shard_map/reduce_scatter | solution.py:48
  367.6 42.0 %copy-start.2 = (f32[384,256]{1,0:T(8,128)S(1)}, f32[384,256]{1,0:T(8,128)}, u32[]{:S(2)}) copy-start(f32[384,256]{1,0:T(8,128)} %reduce-scatter.3.cloned.1.call-done) | copy-start | bytes 1179652
  367.6 421.2 %copy-start.1 = (bf16[256,256]{1,0:T(8,128)(2,1)S(1)}, bf16[256,256]{1,0:T(8,128)(2,1)}, u32[]{:S(2)}) copy-start(bf16[256,256]{1,0:T(8,128)(2,1)} %param.6) | copy-start | bytes 393220
  409.5 377.6 %all-reduce.3.cloned.1.call-start = ((), (), s32[]{:S(2)}) async-start(), calls=%async_computation.5 | async-start | bytes 524288 | tf_op jit(solution)/shard_map/psum | solution.py:42
Sparse Core Ops, SparseCore 0:
  10.7 74.4 all-gather.5
  105.3 141.6 reduce-scatter.2
  250.2 81.6 all-gather.3
  409.6 125.4 reduce-scatter.4
  541.0 246.0 all-reduce.2
where the time goes:
time: 796 us; the launch traced here: 795 us
  waiting for transfers between devices  597 us (75%)
  blocking collectives  71.9 us (9%)
  other arithmetic  48.9 us (6%)
  local copies, waits for them, and re-layouts  33.8 us (4%)
  matrix products  28.7 us (4%)
  between operations  14.5 us (2%)
    psum x1, waiting for transfers between devices, shards(): grad_weight = lax.psum(weight_part, ('rep', 'row'))  250 us
    reduce_scatter x1, waiting for transfers between devices, shards(): lax.psum_scatter(col_sum.reshape(-1, feat_width), 'row', scatter_dimensio...  124 us
    all_gather x1, waiting for transfers between devices, shards(): slab_grad = lax.all_gather(scaled_grad, 'rep', axis=0, tiled=True)  81.5 us
    all_gather x1, waiting for transfers between devices, shards(): gathered = lax.all_gather(features[0], 'row', axis=0, tiled=True)  76.3 us
    unnamed x1, blocking collectives  71.9 us
    reduce_scatter x1, waiting for transfers between devices, shards(): lax.psum_scatter(partial_value, 'rep', scatter_dimension=0, tiled=True)  63.9 us
    scatter-add x1, other arithmetic, shards(): jax.ops.segment_sum(contrib.reshape(-1, tile_size, feat_width), columns.r...  41.9 us
    reshape x1, local copies, waits for them, and re-layouts, shards(): contrib.reshape(-1, tile_size, feat_width)  18.6 us
  transfers between devices with their start and end apart: 5, of which 5 were waited for; matrix products, arithmetic and copies ran while one was open for 1% of the time, Pallas kernels for 0%

commit v1 on v0

v1 whole, which is shorter than its diff:
```python
import jax
import jax.numpy as jnp
from jax import lax
from jax.experimental import pallas as pl
from jax.experimental.pallas import tpu as pltpu
from jax.sharding import PartitionSpec as P

BF16 = jnp.bfloat16
F32 = jnp.float32
MESH = pl.DeviceIdType.MESH
TILE = 128
HALVES = 2
MESSAGES = 160


def order_by_column(columns):
    flat = columns.reshape(-1)
    entry = jnp.arange(flat.shape[0])
    tile = jnp.arange(48)
    before = (flat[None, :] < flat[:, None]) | (
        (flat[None, :] == flat[:, None]) & (entry[None, :] < entry[:, None])
    )
    rank = jnp.sum(before, axis=1)
    onehot = rank[:, None] == entry[None, :]
    perm = jnp.sum(jnp.where(onehot, entry[:, None], 0), axis=0).astype(jnp.int32)
    smaller = jnp.sum(flat[None, :] < flat[:, None], axis=1)
    first = jnp.sum(jnp.where(onehot, (smaller == rank)[:, None], False), axis=0)
    same = 1.0 - first.astype(F32)
    upto = jnp.sum(flat[:, None] <= tile[None, :], axis=0)
    last = jnp.maximum(upto - 1, 0).astype(jnp.int32)
    used = jnp.any(flat[:, None] == tile[None, :], axis=0).astype(F32)
    return flat, perm, same, last, used


def kernel(
    cols, perm, same, last, used, feat_in, weight, cot, counts_hbm,
    act_out, gf_out, gw_out,
    raw, cnt, cnt_t, feats0, feats1, psend0, psend1, yrel, yfin, zsend, zrecv,
    slab0, slab1, prefix, acc, cout0, cout1, corer, xs, xrel, xfin, keep, zfs, zfr,
    deg_send, deg_y, deg_zs, deg_z, agg, gpre,
    wp, g_core, g1, g_x, g2, g_zh, g3, g_y, g4, g_zl, gw_full,
    load_sem, send_sem, recv_sem,
):
    rep = lax.axis_index("rep")
    row = lax.axis_index("row")
    y, zl = rep // 4, rep % 4
    x, zh, c = row // 4, (row // 2) % 2, row % 2
    feats, psend, slab, cout = (
        (feats0, feats1), (psend0, psend1), (slab0, slab1), (cout0, cout1)
    )

    def device(x_=x, y_=y, zl_=zl, zh_=zh, c_=c):
        return (y_ * 4 + zl_, x_ * 4 + zh_ * 2 + c_)

    xp, xm, xo = (x + 1) % 4, (x + 3) % 4, (x + 2) % 4
    yp, ym, yo = (y + 1) % 4, (y + 3) % 4, (y + 2) % 4
    zn = [(zl + d) % 4 for d in range(4)]
    to_xp, to_xm, to_xo = device(x_=xp), device(x_=xm), device(x_=xo)
    to_yp, to_ym, to_yo = device(y_=yp), device(y_=ym), device(y_=yo)
    to_z = [None] + [device(zl_=zn[d]) for d in (1, 2, 3)]
    to_zh = device(zh_=1 - zh)
    to_core = device(c_=1 - c)
    partners = [to_xp, to_xm, to_xo, to_yp, to_ym, to_yo, *to_z[1:], to_zh, to_core]

    sent = {}

    def send(name, src, dst, target):
        slot = len(sent)
        copy = pltpu.make_async_remote_copy(
            src_ref=src, dst_ref=dst, send_sem=send_sem.at[slot], recv_sem=recv_sem.at[slot],
            device_id=target, device_id_type=MESH,
        )
        copy.start()
        sent[name] = copy

    def arrived(name):
        sent[name].wait_recv()

    loads = []
    for i in range(16):
        piece = pl.ds(3 * i, 3)
        load = pltpu.make_async_copy(counts_hbm.at[piece], raw.at[piece], load_sem.at[i])
        load.start()
        loads.append(load)

    barrier = pltpu.get_barrier_semaphore()
    for partner in partners:
        pl.semaphore_signal(barrier, inc=1, device_id=partner, device_id_type=MESH)

    def block(ref, index):
        return ref.at[pl.ds(3 * index, 3)]

    own_row = x * 4 + zh * 2 + c
    for h in range(HALVES):
        feats[h][pl.ds(3 * own_row, 3)] = feat_in[:, :, h * TILE : (h + 1) * TILE]
    pl.semaphore_wait(barrier, len(partners))

    def gather_start(h):
        mine = block(feats[h], own_row)
        send(("xp", h), mine, mine, to_xp)
        send(("xm", h), mine, mine, to_xm)
        send(("zh", h), mine, mine, to_zh)
        send(("c0", h), mine, mine, to_core)

    def row_index(x_, zh_):
        return x_ * 4 + zh_ * 2 + c

    def gather_near(h):
        arrived(("xp", h))
        left = block(feats[h], row_index(xm, zh))
        send(("xp2", h), left, left, to_xp)
        send(("c1", h), left, left, to_core)
        arrived(("xm", h))
        right = block(feats[h], row_index(xp, zh))
        send(("c2", h), right, right, to_core)

    def gather_far(h):
        arrived(("zh", h))
        other = block(feats[h], row_index(x, 1 - zh))
        send(("zxp", h), other, other, to_xp)
        send(("zxm", h), other, other, to_xm)
        send(("c3", h), other, other, to_core)

    def gather_near2(h):
        arrived(("xp2", h))
        oppo = block(feats[h], row_index(xo, zh))
        send(("c4", h), oppo, oppo, to_core)

    def gather_far2(h):
        arrived(("zxm", h))
        right = block(feats[h], row_index(xp, 1 - zh))
        send(("zxm2", h), right, right, to_xm)
        send(("c5", h), right, right, to_core)
        arrived(("zxp", h))
        left = block(feats[h], row_index(xm, 1 - zh))
        send(("c6", h), left, left, to_core)

    def gather_end(h):
        arrived(("zxm2", h))
        oppo = block(feats[h], row_index(xo, 1 - zh))
        send(("c7", h), oppo, oppo, to_core)
        for i in range(8):
            arrived(("c%d" % i, h))

    def convert(first, end):
        for i in range(first, end):
            loads[i].wait()
            for t in range(3):
                total = None
                for k in range(3):
                    tile = raw[3 * i + t, k].astype(F32)
                    cnt[3 * i + t, :, k * TILE : (k + 1) * TILE] = tile.astype(BF16)
                    turned = tile.T
                    cnt_t[9 * i + 3 * t + k] = turned.astype(BF16)
                    part = jnp.sum(turned, axis=0, keepdims=True)
                    total = part if total is None else total + part
                deg_send[i // 4, i % 4, t : t + 1] = total

    def forward(h, target):
        def step(i, carry):
            r = target * 12 + i
            picked = jnp.concatenate([feats[h][cols[3 * r + k]] for k in range(3)], axis=0)
            psend[h][r] = jnp.dot(cnt[r], picked, preferred_element_type=F32).astype(BF16)
            return carry

        lax.fori_loop(0, 12, step, 0, unroll=12)

    def pair(h, target, which):
        return psend[h].at[pl.ds(target * 12 + 6 * which, 6)]

    def add_into(ref, where, other):
        ref[where] = (ref[where].astype(F32) + other.astype(F32)).astype(BF16)

    def reduce_start(h):
        forward(h, yo)
        send(("yr0", h), pair(h, yo, 0), yrel.at[h, 0], to_yp)
        send(("yr1", h), pair(h, yo, 1), yrel.at[h, 1], to_ym)

    def reduce_near(h):
        forward(h, yp)
        send(("yu0", h), pair(h, yp, 1), yfin.at[h, 0, 1], to_yp)
        forward(h, ym)
        send(("yu1", h), pair(h, ym, 0), yfin.at[h, 1, 0], to_ym)

    def reduce_relay(h):
        arrived(("yr0", h))
        add_into(psend[h], pl.ds(yp * 12, 6), yrel[h, 0])
        send(("yc0", h), pair(h, yp, 0), yfin.at[h, 0, 0], to_yp)
        arrived(("yr1", h))
        add_into(psend[h], pl.ds(ym * 12 + 6, 6), yrel[h, 1])
        send(("yc1", h), pair(h, ym, 1), yfin.at[h, 1, 1], to_ym)

    def reduce_z(h):
        for name in ("yu0", "yu1", "yc0", "yc1"):
            arrived((name, h))
        for which in range(2):
            mine = psend[h][pl.ds(y * 12 + 6 * which, 6)].astype(F32)
            total = mine + yfin[h, 0, which].astype(F32) + yfin[h, 1, which].astype(F32)
            zsend[h, pl.ds(2 * which, 2)] = total.astype(BF16).reshape(2, 3, TILE, TILE)
        for d in (1, 2, 3):
            send(("rz%d" % d, h), zsend.at[h, zn[d]], zrecv.at[h, zl], to_z[d])

    def degree_start():
        deg_y[y] = deg_send[y]
        for name, target, index in (("dp", to_yp, yp), ("dm", to_ym, ym), ("do", to_yo, yo)):
            send(name, deg_send.at[index], deg_y.at[y], target)

    def degree_z():
        for name in ("dp", "dm", "do"):
            arrived(name)
        deg_zs[...] = deg_y[0] + deg_y[1] + deg_y[2] + deg_y[3]
        deg_z[zl] = deg_zs[zl]
        for d in (1, 2, 3):
            send("dz%d" % d, deg_zs.at[zn[d]], deg_z.at[zl], to_z[d])

    def degree_end():
        for d in (1, 2, 3):
            arrived("dz%d" % d)
        total = deg_z[0] + deg_z[1] + deg_z[2] + deg_z[3]
        return lax.rsqrt(1.0 + total)

    own_rep = y * 4 + zl

    def dense(scale):
        for h in range(HALVES):
            for d in (1, 2, 3):
                arrived(("rz%d" % d, h))
        for t in range(3):
            column = jnp.broadcast_to(scale[t : t + 1], (TILE, TILE)).T
            halves = []
            for h in range(HALVES):
                total = zsend[h, zl, t].astype(F32)
                for d in (1, 2, 3):
                    total = total + zrecv[h, zn[d], t].astype(F32)
                halves.append((total * column).astype(BF16))
            aggregated = jnp.concatenate(halves, axis=1)
            rows = pl.ds(t * TILE, TILE)
            agg[rows] = aggregated
            preact = jnp.dot(aggregated, weight[...], preferred_element_type=F32)
            gate = jax.nn.sigmoid(preact)
            act_out[rows] = (preact * gate).astype(BF16)
            grad = (cot[rows].astype(F32) * gate * (1.0 + preact * (1.0 - gate))).astype(BF16)
            gpre[rows] = grad
            back = lax.dot_general(
                grad, weight[...], (((1,), (1,)), ((), ())), preferred_element_type=F32
            )
            for h in range(HALVES):
                part = back[:, h * TILE : (h + 1) * TILE] * column
                slab[h][3 * own_rep + t] = part.astype(BF16)

    def spread_start(h):
        mine = block(slab[h], own_rep)
        send(("sp0", h), mine, mine, to_yp)
        send(("sm0", h), mine, mine, to_ym)
        for d in (1, 2, 3):
            send(("sz%d" % d, h), mine, mine, to_z[d])

    def spread_z(h, d):
        arrived(("sz%d" % d, h))
        got = block(slab[h], y * 4 + zn[4 - d])
        send(("sp%d" % d, h), got, got, to_yp)
        send(("sm%d" % d, h), got, got, to_ym)

    def spread_y(h, d):
        source = zl if d == 0 else zn[4 - d]
        arrived(("sp%d" % d, h))
        if d % 2 == 0:
            got = block(slab[h], ym * 4 + source)
            send(("sf%d" % d, h), got, got, to_yp)
        arrived(("sm%d" % d, h))
        if d % 2 == 1:
            got = block(slab[h], yp * 4 + source)
            send(("sf%d" % d, h), got, got, to_ym)

    def spread_end(h):
        for d in range(4):
            arrived(("sf%d" % d, h))

    def backward(h, first, end):
        def step(i, carry):
            e = perm[i]
            part = jnp.dot(cnt_t[e], slab[h][e // 3], preferred_element_type=F32)
            total = acc[...] * same[i] + part
            acc[...] = total
            prefix[i] = total.astype(BF16)
            return carry

        lax.fori_loop(first, end, step, 0, unroll=12)

    def collect(h):
        def step(i, carry):
            for t in range(3):
                j = 3 * i + t
                tile = prefix[last[j]].astype(F32) * used[j]
                cout[h][i // 2, i % 2, t] = tile.astype(BF16)
            return carry

        lax.fori_loop(0, 16, step, 0, unroll=4)

    def core_start(h):
        for name, x_ in (("o", xo), ("p", xp), ("m", xm), ("s", x)):
            send(
                ("k" + name, h), cout[h].at[pl.ds(2 * x_, 2), 1 - c],
                corer.at[h, pl.ds(2 * x_, 2)], to_core,
            )

    def core_sum(h, name, x_):
        arrived(("k" + name, h))
        pieces = pl.ds(2 * x_, 2)
        total = cout[h][pieces, c].astype(F32) + corer[h, pieces].astype(F32)
        xs[h, pieces] = total.astype(BF16)

    def cross_start(h):
        core_sum(h, "o", xo)
        send(("xr0", h), xs.at[h, 2 * xo], xrel.at[h, 0], to_xp)
        send(("xr1", h), xs.at[h, 2 * xo + 1], xrel.at[h, 1], to_xm)
        core_sum(h, "p", xp)
        send(("xu0", h), xs.at[h, 2 * xp + 1], xfin.at[h, 0, 1], to_xp)
        core_sum(h, "m", xm)
        send(("xu1", h), xs.at[h, 2 * xm], xfin.at[h, 1, 0], to_xm)
        core_sum(h, "s", x)

    def cross_relay(h):
        arrived(("xr0", h))
        add_into(xs, (h, 2 * xp), xrel[h, 0])
        send(("xc0", h), xs.at[h, 2 * xp], xfin.at[h, 0, 0], to_xp)
        arrived(("xr1", h))
        add_into(xs, (h, 2 * xm + 1), xrel[h, 1])
        send(("xc1", h), xs.at[h, 2 * xm + 1], xfin.at[h, 1, 1], to_xm)

    def cross_sum(h, which):
        return (
            xs[h, 2 * x + which].astype(F32)
            + xfin[h, 0, which].astype(F32)
            + xfin[h, 1, which].astype(F32)
        )

    def cross_z(h):
        for name in ("xu0", "xu1", "xc0", "xc1"):
            arrived((name, h))
        zfs[h] = cross_sum(h, 1 - zh).astype(BF16)
        send(("fz", h), zfs.at[h], zfr.at[h], to_zh)
        keep[h] = cross_sum(h, zh)

    def cross_end(h):
        arrived(("fz", h))
        total = keep[h] + zfr[h].astype(F32)
        gf_out[:, :, h * TILE : (h + 1) * TILE] = total.astype(BF16)

    def gw_start():
        part = lax.dot_general(
            agg[...], gpre[...], (((0,), (0,)), ((), ())), preferred_element_type=F32
        )
        wp[...] = part.reshape(2, 4, 2, 16, 256)
        send("gc", wp.at[1 - c], g_core, to_core)

    def gw_x():
        arrived("gc")
        g1[...] = wp[c] + g_core[...]
        g_x[x] = g1[x]
        for name, target, x_ in (("gxp", to_xp, xp), ("gxm", to_xm, xm), ("gxo", to_xo, xo)):
            send(name, g1.at[x_], g_x.at[x], target)

    def gw_zh():
        for name in ("gxp", "gxm", "gxo"):
            arrived(name)
        g2[...] = g_x[0] + g_x[1] + g_x[2] + g_x[3]
        send("gzh", g2.at[1 - zh], g_zh, to_zh)

    def gw_y():
        arrived("gzh")
        g3[...] = g2[zh] + g_zh[...]
        g_y[y] = g3[...]
        for name, target in (("gyp", to_yp), ("gym", to_ym), ("gyo", to_yo)):
            send(name, g3, g_y.at[y], target)

    def gw_zl():
        for name in ("gyp", "gym", "gyo"):
            arrived(name)
        g4[...] = g_y[0] + g_y[1] + g_y[2] + g_y[3]
        g_zl[zl] = g4[...]
        for d in (1, 2, 3):
            send("gzl%d" % d, g4, g_zl.at[zl], to_z[d])

    def gw_back_zh():
        for d in (1, 2, 3):
            arrived("gzl%d" % d)
        gw_full[c, x, zh] = g_zl[0] + g_zl[1] + g_zl[2] + g_zl[3]
        mine = gw_full.at[c, x, zh]
        send("bzh", mine, mine, to_zh)

    def gw_back_x():
        arrived("bzh")
        mine = gw_full.at[c, x]
        for name, target in (("bxp", to_xp), ("bxm", to_xm), ("bxo", to_xo)):
            send(name, mine, mine, target)

    def gw_back_core():
        for name in ("bxp", "bxm", "bxo"):
            arrived(name)
        mine = gw_full.at[c]
        send("bc", mine, mine, to_core)

    def gw_end():
        arrived("bc")
        gw_out[...] = gw_full[...].reshape(256, 256)

    gather_start(0)
    gather_start(1)
    convert(0, 5)
    gather_near(0)
    convert(5, 10)
    gather_near2(0)
    gather_near(1)
    gather_far(0)
    convert(10, 16)
    degree_start()
    gather_near2(1)
    gather_far2(0)
    degree_z()
    gather_far(1)
    gather_end(0)

    reduce_start(0)
    gather_far2(1)
    reduce_near(0)
    forward(0, y)
    gather_end(1)
    reduce_start(1)
    reduce_relay(0)
    reduce_near(1)
    forward(1, y)
    scale = degree_end()
    reduce_z(0)
    reduce_relay(1)
    reduce_z(1)
    dense(scale)

    spread_start(0)
    spread_start(1)
    gw_start()
    acc[...] = jnp.zeros_like(acc)
    spread_y(0, 0)
    spread_z(0, 1)
    spread_y(1, 0)
    gw_x()
    spread_z(0, 2)
    spread_y(0, 1)
    spread_z(0, 3)
    spread_y(0, 2)
    gw_zh()
    spread_z(1, 1)
    spread_y(0, 3)
    spread_z(1, 2)
    spread_end(0)
    backward(0, 0, 72)
    spread_y(1, 1)
    spread_z(1, 3)
    backward(0, 72, 144)
    collect(0)
    core_start(0)
    spread_y(1, 2)
    cross_start(0)
    gw_y()
    spread_y(1, 3)
    cross_relay(0)
    spread_end(1)
    backward(1, 0, 72)
    gw_zl()
    backward(1, 72, 108)
    cross_z(0)
    backward(1, 108, 144)
    collect(1)
    core_start(1)
    gw_back_zh()
    cross_start(1)
    gw_back_x()
    cross_relay(1)
    gw_back_core()
    cross_end(0)
    cross_z(1)
    gw_end()
    cross_end(1)
    for copy in sent.values():
        copy.wait_send()


def shards(features, weight, block_cols, edge_counts, cotangent):
    cols, perm, same, last, used = order_by_column(block_cols[0])
    vmem = pl.BlockSpec(memory_space=pltpu.VMEM)
    smem = pl.BlockSpec(memory_space=pltpu.SMEM)
    slab = pltpu.VMEM((48, TILE, TILE), BF16)

    def tiles(*lead, dtype=BF16):
        return pltpu.VMEM((*lead, TILE, TILE), dtype)

    def floats(*shape):
        return pltpu.VMEM(shape, F32)

    activated, grad_features, grad_weight = pl.pallas_call(
        kernel,
        out_shape=(
            jax.ShapeDtypeStruct((384, 256), BF16),
            jax.ShapeDtypeStruct((3, TILE, 256), BF16),
            jax.ShapeDtypeStruct((256, 256), F32),
        ),
        in_specs=[smem] * 5 + [vmem] * 3 + [pl.BlockSpec(memory_space=pl.ANY)],
        out_specs=(vmem, vmem, vmem),
        scratch_shapes=[
            tiles(48, 3, dtype=jnp.int32),
            pltpu.VMEM((48, TILE, 3 * TILE), BF16),
            tiles(144),
            slab, slab, slab, slab,
            tiles(2, 2, 6),
            tiles(2, 2, 2, 6),
            tiles(2, 4, 3), tiles(2, 4, 3),
            slab, slab,
            tiles(144),
            floats(TILE, TILE),
            tiles(8, 2, 3), tiles(8, 2, 3),
            tiles(2, 8, 3), tiles(2, 8, 3),
            tiles(2, 2, 3), tiles(2, 2, 2, 3),
            tiles(2, 3, dtype=F32), tiles(2, 3), tiles(2, 3),
            floats(4, 4, 8, TILE), floats(4, 4, 8, TILE),
            floats(4, 8, TILE), floats(4, 8, TILE),
            pltpu.VMEM((384, 256), BF16), pltpu.VMEM((384, 256), BF16),
            floats(2, 4, 2, 16, 256),
            floats(4, 2, 16, 256), floats(4, 2, 16, 256),
            floats(4, 2, 16, 256), floats(2, 16, 256),
            floats(16, 256), floats(16, 256),
            floats(4, 16, 256), floats(16, 256),
            floats(4, 16, 256),
            floats(2, 4, 2, 16, 256),
            pltpu.SemaphoreType.DMA((16,)),
            pltpu.SemaphoreType.DMA((MESSAGES,)),
            pltpu.SemaphoreType.DMA((MESSAGES,)),
        ],
        compiler_params=pltpu.CompilerParams(
            collective_id=0, has_side_effects=True, vmem_limit_bytes=60 << 20
        ),
        name="graph_layer",
    )(
        cols, perm, same, last, used,
        features[0].reshape(3, TILE, 256), weight, cotangent[0], edge_counts[0],
    )
    return activated[None], grad_features.reshape(1, 384, 256), grad_weight


def solution(mesh):
    placed = (
        P("rep", "row", None),
        P(),
        P("rep", "row", None),
        P("rep", "row", None, None, None),
        P("row", "rep", None),
    )
    return jax.shard_map(
        shards,
        mesh=mesh,
        in_specs=placed,
        out_specs=(P("row", "rep", None), P("rep", "row", None), P()),
        check_vma=False,
    )
```

time: 796 us -> 144 us (0.18)
  the two profiles are of different devices: /device:TPU:1 before, /device:TPU:49 now
where the time goes in v1:
time: 144 us; the launch traced here: 143 us
  Pallas kernels  134 us (93%)
  local copies, waits for them, and re-layouts  5.79 us (4%)
  other arithmetic  2.82 us (2%)
    pallas_call x1, Pallas kernels, shards(): pl.pallas_call(kernel, out_shape=(jax.ShapeDtypeStruct((384, 256), BF16),...  134 us
    unnamed x6, local copies, waits for them, and re-layouts  5.67 us

profile of v1, /device:TPU:49, one launch (start us, length us, event | category | flops | bytes accessed | tf_op | source)
XLA Modules:
  0.0 143.5 jit_solution(11875534720239475617)
XLA Ops:
  0.6 0.8 copy.9
  1.4 0.1 reshape_squeeze.6.cols
  1.5 0.0 copy-start
  1.5 0.1 convert_reduce_fusion.2
  1.6 0.5 add_maximum_fusion.last
  2.2 0.1 fusion.3
  2.3 0.6 convert_element_type.23.used
  2.9 0.2 fusion
  3.1 0.7 convert_reduce_fusion
  3.8 0.6 convert_subtract_fusion.same
  4.4 0.0 copy-done
  4.4 134.2 %graph_layer.1 = (bf16[384,256]{1,0:T(8,128)(2,1)}, bf16[3,128,256]{2,1,0:T(8,128)(2,1)}, f32[256,256]{1,0:T(8,128)}) custom-call(s32[144]{0:T(256)} %copy-done, s32[144]{0:T(256)} %get-tuple-element.10.perm, f32[144]{0:T(256)} %convert_subtract_fusion.same, s32[48]{0:T(128)} %add_maximum_fusion.last, f32[48]{0:T(128)} %convert_element_type.23.used, ...), custom_call_target="tpu_custom_call" | custom-call | tf_op jit(solution)/shard_map/graph_layer/pallas_call | solution.py:500
  138.6 1.6 %copy.13 = bf16[1,384,256]{2,1,0:T(8,128)(2,1)} copy(bf16[1,384,256]{2,1,0:T(8,128)(2,1)} %bitcast.7) | data formatting | bytes 393216
  140.2 1.6 %copy.14 = bf16[1,384,256]{2,1,0:T(8,128)(2,1)} copy(bf16[1,384,256]{2,1,0:T(8,128)(2,1)} %bitcast.6) | data formatting | bytes 393216
  141.8 1.7 %copy.15 = f32[256,256]{1,0:T(8,128)} copy(f32[256,256]{1,0:T(8,128)} %get-tuple-element.18) | data formatting | bytes 524288
  (1 shorter events, 0.0 us)
Async XLA Ops:
  1.5 2.8 %copy-start = (s32[144]{0:T(256)}, s32[144]{0:T(256)S(1)}, u32[]{:S(2)}) copy-start(s32[144]{0:T(256)S(1)} %reshape_squeeze.6.cols) | copy-start | bytes 1732

commit v2 on v1

v2 whole, which is shorter than its diff:
```python
import jax
import jax.numpy as jnp
from jax import lax
from jax.experimental import pallas as pl
from jax.experimental.pallas import tpu as pltpu
from jax.sharding import PartitionSpec as P

BF16 = jnp.bfloat16
F32 = jnp.float32
MESH = pl.DeviceIdType.MESH
TILE = 128
HALVES = 2
MESSAGES = 192
SUM_PARTS = ((0, 0, 3), (1, 0, 1), (1, 1, 2))
SPREAD_PARTS = ((0, 0, 1), (1, 0, 1), (0, 1, 2), (1, 1, 2))


def kernel(
    cols, cols_in, feat_hbm, weight_hbm, cot_hbm, counts_hbm,
    act_hbm, gf_hbm, gw_hbm,
    raw, cnt, cnt_t, feats0, feats1, psend0, psend1, pown, yrel, yfin, zsend, zown, zrecv,
    slab0, slab1, prefix, acc, cout0, cout1, corer, xs, xown, xfin, keep, zfs, zfr,
    deg_send, deg_y, deg_zs, deg_z, weight, cot, act, agg, gpre, gf,
    wp, g_core, g1, g_x, g2, g_zh, g3, g_y, g4, g_zl, gw_full,
    order_v, flag_v, order, flag,
    load_sem, late_sem, send_sem, recv_sem,
):
    rep = lax.axis_index("rep")
    row = lax.axis_index("row")
    y, zl = rep // 4, rep % 4
    x, zh, c = row // 4, (row // 2) % 2, row % 2
    feats, psend, slab, cout = (
        (feats0, feats1), (psend0, psend1), (slab0, slab1), (cout0, cout1)
    )

    def device(x_=x, y_=y, zl_=zl, zh_=zh, c_=c):
        return (y_ * 4 + zl_, x_ * 4 + zh_ * 2 + c_)

    xp, xm, xo = (x + 1) % 4, (x + 3) % 4, (x + 2) % 4
    yp, ym, yo = (y + 1) % 4, (y + 3) % 4, (y + 2) % 4
    zn = [(zl + d) % 4 for d in range(4)]
    to_xp, to_xm, to_xo = device(x_=xp), device(x_=xm), device(x_=xo)
    to_yp, to_ym, to_yo = device(y_=yp), device(y_=ym), device(y_=yo)
    to_z = [None] + [device(zl_=zn[d]) for d in (1, 2, 3)]
    to_zh = device(zh_=1 - zh)
    to_core = device(c_=1 - c)
    partners = [to_xp, to_xm, to_xo, to_yp, to_ym, to_yo, *to_z[1:], to_zh, to_core]

    sent = {}

    def send(name, src, dst, target):
        slot = len(sent)
        copy = pltpu.make_async_remote_copy(
            src_ref=src, dst_ref=dst, send_sem=send_sem.at[slot], recv_sem=recv_sem.at[slot],
            device_id=target, device_id_type=MESH,
        )
        copy.start()
        sent[name] = copy

    def arrived(name):
        sent[name].wait_recv()

    barrier = pltpu.get_barrier_semaphore()
    for partner in partners:
        pl.semaphore_signal(barrier, inc=1, device_id=partner, device_id_type=MESH)

    def block(ref, index):
        return ref.at[pl.ds(3 * index, 3)]

    own_row = x * 4 + zh * 2 + c
    own_rep = y * 4 + zl

    early = []
    for h in range(HALVES):
        early.append(
            pltpu.make_async_copy(
                feat_hbm.at[:, :, pl.ds(h * TILE, TILE)], block(feats[h], own_row), late_sem.at[h]
            )
        )
    loads = []
    for i in range(16):
        piece = pl.ds(3 * i, 3)
        loads.append(pltpu.make_async_copy(counts_hbm.at[piece], raw.at[piece], load_sem.at[i]))
    late = [
        pltpu.make_async_copy(weight_hbm, weight, late_sem.at[2]),
        pltpu.make_async_copy(cot_hbm, cot, late_sem.at[3]),
    ]
    for copy in early + loads + late:
        copy.start()
    out = []

    def put(src, dst, slot):
        copy = pltpu.make_async_copy(src, dst, late_sem.at[slot])
        copy.start()
        out.append(copy)

    for copy in early:
        copy.wait()
    pl.semaphore_wait(barrier, len(partners))

    def gather_z(h):
        mine = block(feats[h], own_row)
        send(("zh", h), mine, mine, to_zh)

    def gather_start(h):
        mine = block(feats[h], own_row)
        send(("xp", h), mine, mine, to_xp)
        send(("xm", h), mine, mine, to_xm)
        send(("c0", h), mine, mine, to_core)

    def row_index(x_, zh_):
        return x_ * 4 + zh_ * 2 + c

    def gather_near(h):
        arrived(("xp", h))
        left = block(feats[h], row_index(xm, zh))
        send(("xp2", h), left, left, to_xp)
        send(("c1", h), left, left, to_core)
        arrived(("xm", h))
        right = block(feats[h], row_index(xp, zh))
        send(("c2", h), right, right, to_core)

    def gather_far(h):
        arrived(("zh", h))
        other = block(feats[h], row_index(x, 1 - zh))
        send(("zxo", h), other, other, to_xo)
        send(("zxp", h), other, other, to_xp)
        send(("zxm", h), other, other, to_xm)
        send(("c3", h), other, other, to_core)

    def gather_near2(h):
        arrived(("xp2", h))
        oppo = block(feats[h], row_index(xo, zh))
        send(("c4", h), oppo, oppo, to_core)

    def gather_far2(h):
        for name, x_ in (("zxm", xp), ("zxp", xm), ("zxo", xo)):
            arrived((name, h))
            got = block(feats[h], row_index(x_, 1 - zh))
            send(("c" + name, h), got, got, to_core)

    def gather_end(h):
        for name in ("c0", "c1", "c2", "c3", "c4", "czxm", "czxp", "czxo"):
            arrived((name, h))

    def convert(first, end):
        for i in range(first, end):
            loads[i].wait()
            for t in range(3):
                total = None
                for k in range(3):
                    tile = raw[3 * i + t, k].astype(F32)
                    cnt[3 * i + t, :, k * TILE : (k + 1) * TILE] = tile.astype(BF16)
                    turned = tile.T
                    cnt_t[48 * k + 3 * i + t] = turned.astype(BF16)
                    part = jnp.sum(turned, axis=0, keepdims=True)
                    total = part if total is None else total + part
                deg_send[i // 4, i % 4, t : t + 1] = total

    def sort_tiles():
        side = 256
        line = jnp.concatenate(
            [cols_in[k] for k in range(3)] + [jnp.full((1, side - 144), 1000, jnp.int32)], axis=1
        )
        along = jnp.broadcast_to(line, (side, side))
        down = along.T
        at_row = lax.broadcasted_iota(jnp.int32, (side, side), 0)
        at_col = lax.broadcasted_iota(jnp.int32, (side, side), 1)
        less = (along < down).astype(jnp.int32)
        tied = ((along == down) & (at_col < at_row)).astype(jnp.int32)
        smaller = jnp.sum(less, axis=1, keepdims=True)
        rank = smaller + jnp.sum(tied, axis=1, keepdims=True)
        here = (rank == at_col).astype(jnp.int32)
        entry = at_row
        block_row = at_row - 48 * ((at_row >= 48).astype(jnp.int32) + (at_row >= 96).astype(jnp.int32))
        first = jnp.broadcast_to((smaller == rank).astype(jnp.int32), (side, side))

        def total(value):
            return jnp.sum(value, axis=0, keepdims=True)

        upto = total((down <= at_col).astype(jnp.int32))
        below = total((down < at_col).astype(jnp.int32))
        order_v[0:1] = total(here * entry)
        order_v[1:2] = total(here * block_row)
        order_v[2:3] = jnp.maximum(upto - 1, 0)
        flag_v[0:1] = 1.0 - total(here * first).astype(F32)
        flag_v[1:2] = jnp.minimum(upto - below, 1).astype(F32)
        for src, dst, slot in ((order_v, order, 4), (flag_v, flag, 5)):
            put(src, dst, slot)

    def sort_end():
        for copy in out:
            copy.wait()
        out.clear()

    def forward(part, target, own=False):
        h, t0, nt = part

        def step(i, carry):
            which, t = i // nt, t0 + i % nt
            r = target * 12 + which * 3 + t
            picked = jnp.concatenate([feats[h][cols[k, 0, r]] for k in range(3)], axis=0)
            total = jnp.dot(cnt[r], picked, preferred_element_type=F32)
            if own:
                pown[h, which, t] = total
            else:
                psend[h][target * 4 + which, t] = total.astype(BF16)
            return carry

        lax.fori_loop(0, 4 * nt, step, 0, unroll=4 * nt)

    def pair(part, target, which):
        h, t0, nt = part
        return psend[h].at[pl.ds(target * 4 + 2 * which, 2), pl.ds(t0, nt)]

    def add_into(ref, where, other):
        ref[where] = (ref[where].astype(F32) + other.astype(F32)).astype(BF16)

    def relay_in(part, way):
        h, t0, nt = part
        return yrel.at[h, way, :, pl.ds(t0, nt)]

    def final_in(part, way, which):
        h, t0, nt = part
        return yfin.at[h, way, pl.ds(2 * which, 2), pl.ds(t0, nt)]

    def reduce_start(part):
        forward(part, yo)
        send(("yr0", part), pair(part, yo, 0), relay_in(part, 0), to_yp)
        send(("yr1", part), pair(part, yo, 1), relay_in(part, 1), to_ym)

    def reduce_near(part):
        forward(part, yp)
        send(("yu0", part), pair(part, yp, 1), final_in(part, 0, 1), to_yp)
        forward(part, ym)
        send(("yu1", part), pair(part, ym, 0), final_in(part, 1, 0), to_ym)

    def reduce_own(part):
        forward(part, y, own=True)

    def reduce_relay(part):
        h, t0, nt = part
        tiles = pl.ds(t0, nt)
        arrived(("yr0", part))
        add_into(psend[h], (pl.ds(yp * 4, 2), tiles), yrel[h, 0, :, tiles])
        send(("yc0", part), pair(part, yp, 0), final_in(part, 0, 0), to_yp)
        arrived(("yr1", part))
        add_into(psend[h], (pl.ds(ym * 4 + 2, 2), tiles), yrel[h, 1, :, tiles])
        send(("yc1", part), pair(part, ym, 1), final_in(part, 1, 1), to_ym)

    def reduce_z(part):
        h, t0, nt = part
        tiles = pl.ds(t0, nt)
        for name in ("yu0", "yu1", "yc0", "yc1"):
            arrived((name, part))
        for which in range(4):
            total = (
                pown[h, which, tiles]
                + yfin[h, 0, which, tiles].astype(F32)
                + yfin[h, 1, which, tiles].astype(F32)
            )
            zown[h, which, tiles] = total
            zsend[h, which, tiles] = total.astype(BF16)
        for d in (2, 1, 3):
            send(
                ("rz%d" % d, part), zsend.at[h, zn[d], tiles], zrecv.at[h, zl, tiles], to_z[d]
            )

    def degree_start():
        deg_y[y] = deg_send[y]
        for name, target, index in (("dp", to_yp, yp), ("dm", to_ym, ym), ("do", to_yo, yo)):
            send(name, deg_send.at[index], deg_y.at[y], target)

    def degree_z():
        for name in ("dp", "dm", "do"):
            arrived(name)
        deg_zs[...] = deg_y[0] + deg_y[1] + deg_y[2] + deg_y[3]
        deg_z[zl] = deg_zs[zl]
        for d in (1, 2, 3):
            send("dz%d" % d, deg_zs.at[zn[d]], deg_z.at[zl], to_z[d])

    def degree_end():
        for d in (1, 2, 3):
            arrived("dz%d" % d)
        total = deg_z[0] + deg_z[1] + deg_z[2] + deg_z[3]
        return lax.rsqrt(1.0 + total)

    def split(value):
        high = value.astype(BF16)
        return high, (value - high.astype(F32)).astype(BF16)

    def dense_wait(part):
        for d in (1, 2, 3):
            arrived(("rz%d" % d, part))

    def dense(scale, first, end):
        for t in range(first, end):
            column = jnp.broadcast_to(scale[t : t + 1], (TILE, TILE)).T
            halves = []
            for h in range(HALVES):
                total = zown[h, zl, t]
                for d in (1, 2, 3):
                    total = total + zrecv[h, zn[d], t].astype(F32)
                halves.append(total * column)
            high, low = split(jnp.concatenate(halves, axis=1))
            rows = pl.ds(t * TILE, TILE)
            agg[rows] = high
            preact = jnp.dot(high, weight[...], preferred_element_type=F32) + jnp.dot(
                low, weight[...], preferred_element_type=F32
            )
            gate = jax.nn.sigmoid(preact)
            act[rows] = (preact * gate).astype(BF16)
            grad = cot[rows].astype(F32) * gate * (1.0 + preact * (1.0 - gate))
            high, low = split(grad)
            gpre[rows] = high
            turned = (((1,), (1,)), ((), ()))
            back = lax.dot_general(
                high, weight[...], turned, preferred_element_type=F32
            ) + lax.dot_general(low, weight[...], turned, preferred_element_type=F32)
            for h in range(HALVES):
                piece = back[:, h * TILE : (h + 1) * TILE] * column
                slab[h][3 * own_rep + t] = piece.astype(BF16)

    def dense_end():
        put(act, act_hbm, 6)

    def chunk(part, index):
        h, t0, nt = part
        return slab[h].at[pl.ds(3 * index + t0, nt)]

    def spread_start(part):
        mine = chunk(part, own_rep)
        for d in (2, 1, 3):
            send(("sz%d" % d, part), mine, mine, to_z[d])
        send(("sp0", part), mine, mine, to_yp)
        send(("sm0", part), mine, mine, to_ym)

    def spread_z(part, d):
        arrived(("sz%d" % d, part))
        got = chunk(part, y * 4 + zn[4 - d])
        send(("sp%d" % d, part), got, got, to_yp)
        send(("sm%d" % d, part), got, got, to_ym)

    def spread_y(part, d):
        source = zl if d == 0 else zn[4 - d]
        arrived(("sp%d" % d, part))
        if d % 2 == 0:
            got = chunk(part, ym * 4 + source)
            send(("sf%d" % d, part), got, got, to_yp)
        arrived(("sm%d" % d, part))
        if d % 2 == 1:
            got = chunk(part, yp * 4 + source)
            send(("sf%d" % d, part), got, got, to_ym)

    def spread_end(part):
        for d in range(4):
            arrived(("sf%d" % d, part))

    def backward(h, first, end):
        def step(i, carry):
            part = jnp.dot(
                cnt_t[order[0, i]], slab[h][order[1, i]], preferred_element_type=F32
            )
            total = acc[...] * flag[0, i] + part
            acc[...] = total
            prefix[i] = total.astype(BF16)
            return carry

        lax.fori_loop(first, end, step, 0, unroll=12)

    def collect(h):
        def step(i, carry):
            for t in range(3):
                j = 3 * i + t
                tile = prefix[order[2, j]].astype(F32) * flag[1, j]
                cout[h][i // 4, (i // 2) % 2, i % 2, t] = tile.astype(BF16)
            return carry

        lax.fori_loop(0, 16, step, 0, unroll=4)

    planes = (1 - zh, zh)

    def core_start(h):
        for n, plane in enumerate(planes):
            send(
                ("k%d" % n, h), cout[h].at[:, plane, 1 - c], corer.at[h, plane], to_core
            )

    def cross_start(h, n):
        plane = planes[n]
        arrived(("k%d" % n, h))
        total = cout[h][:, plane, c].astype(F32) + corer[h, plane].astype(F32)
        xs[h, plane] = total.astype(BF16)
        xown[h, n] = cout[h][x, plane, c].astype(F32) + corer[h, plane, x].astype(F32)
        for way, target, x_ in ((2, to_xo, xo), (0, to_xp, xp), (1, to_xm, xm)):
            send(("x%d%d" % (way, n), h), xs.at[h, plane, x_], xfin.at[h, n, way], target)

    def cross_sum(h, n):
        for way in (0, 1, 2):
            arrived(("x%d%d" % (way, n), h))
        total = xown[h, n]
        for way in range(3):
            total = total + xfin[h, n, way].astype(F32)
        return total

    def cross_z(h):
        zfs[h] = cross_sum(h, 0).astype(BF16)
        send(("fz", h), zfs.at[h], zfr.at[h], to_zh)

    def cross_own(h):
        keep[h] = cross_sum(h, 1)

    def cross_end(h):
        arrived(("fz", h))
        total = keep[h] + zfr[h].astype(F32)
        gf[h] = total.astype(BF16)
        put(gf.at[h], gf_hbm.at[:, :, pl.ds(h * TILE, TILE)], 8 + h)

    def gw_start():
        part = lax.dot_general(
            agg[...], gpre[...], (((0,), (0,)), ((), ())), preferred_element_type=F32
        )
        wp[...] = part.reshape(2, 4, 2, 16, 256)
        send("gc", wp.at[1 - c], g_core, to_core)

    def gw_x():
        arrived("gc")
        g1[...] = wp[c] + g_core[...]
        g_x[x] = g1[x]
        for name, target, x_ in (("gxp", to_xp, xp), ("gxm", to_xm, xm), ("gxo", to_xo, xo)):
            send(name, g1.at[x_], g_x.at[x], target)

    def gw_zh():
        for name in ("gxp", "gxm", "gxo"):
            arrived(name)
        g2[...] = g_x[0] + g_x[1] + g_x[2] + g_x[3]
        send("gzh", g2.at[1 - zh], g_zh, to_zh)

    def gw_y():
        arrived("gzh")
        g3[...] = g2[zh] + g_zh[...]
        g_y[y] = g3[...]
        for name, target in (("gyp", to_yp), ("gym", to_ym), ("gyo", to_yo)):
            send(name, g3, g_y.at[y], target)

    def gw_zl():
        for name in ("gyp", "gym", "gyo"):
            arrived(name)
        g4[...] = g_y[0] + g_y[1] + g_y[2] + g_y[3]
        g_zl[zl] = g4[...]
        for d in (1, 2, 3):
            send("gzl%d" % d, g4, g_zl.at[zl], to_z[d])

    def gw_back_zh():
        for d in (1, 2, 3):
            arrived("gzl%d" % d)
        gw_full[c, x, zh] = g_zl[0] + g_zl[1] + g_zl[2] + g_zl[3]
        mine = gw_full.at[c, x, zh]
        send("bzh", mine, mine, to_zh)

    def gw_back_x():
        arrived("bzh")
        mine = gw_full.at[c, x]
        for name, target in (("bxp", to_xp), ("bxm", to_xm), ("bxo", to_xo)):
            send(name, mine, mine, target)

    def gw_back_core():
        for name in ("bxp", "bxm", "bxo"):
            arrived(name)
        mine = gw_full.at[c]
        send("bc", mine, mine, to_core)

    def gw_end():
        arrived("bc")
        put(gw_full, gw_hbm, 7)

    s0, s1, s2 = SUM_PARTS
    a0, a1, b0, b1 = SPREAD_PARTS
    gather_z(0)
    gather_start(0)
    convert(0, 5)
    gather_z(1)
    gather_start(1)
    convert(5, 10)
    gather_near(0)
    convert(10, 16)
    gather_far(0)
    gather_near2(0)
    gather_near(1)
    degree_start()
    gather_far(1)
    gather_near2(1)
    gather_far2(0)
    gather_end(0)
    reduce_start(s0)
    reduce_near(s0)
    gather_far2(1)
    reduce_own(s0)
    degree_z()
    reduce_relay(s0)
    gather_end(1)
    reduce_start(s1)
    reduce_near(s1)
    reduce_start(s2)
    reduce_own(s1)
    reduce_relay(s1)
    reduce_near(s2)
    reduce_own(s2)
    reduce_z(s0)
    reduce_relay(s2)
    sort_tiles()
    scale = degree_end()
    for copy in late:
        copy.wait()
    sort_end()
    acc[...] = jnp.zeros_like(acc)
    reduce_z(s1)
    dense_wait(s0)
    dense_wait(s1)
    dense(scale, 0, 1)
    spread_start(a0)
    spread_start(a1)
    reduce_z(s2)
    spread_y(a0, 0)
    spread_y(a1, 0)
    for d in (1, 2, 3):
        spread_z(a0, d)
        spread_z(a1, d)
    dense_wait(s2)
    dense(scale, 1, 3)
    spread_start(b0)
    spread_start(b1)
    dense_end()
    for d in (1, 2, 3):
        spread_y(a0, d)
        spread_y(a1, d)
    gw_start()
    spread_y(b0, 0)
    for d in (1, 2, 3):
        spread_z(b0, d)
    spread_y(b1, 0)
    gw_x()
    for d in (1, 2, 3):
        spread_z(b1, d)
    for d in (1, 2, 3):
        spread_y(b0, d)
    gw_zh()
    spread_end(a0)
    spread_end(a1)
    spread_end(b0)
    backward(0, 0, 36)
    spread_y(b1, 1)
    backward(0, 36, 72)
    spread_y(b1, 2)
    backward(0, 72, 108)
    spread_y(b1, 3)
    backward(0, 108, 144)
    collect(0)
    core_start(0)
    gw_y()
    spread_end(b1)
    backward(1, 0, 36)
    cross_start(0, 0)
    cross_start(0, 1)
    backward(1, 36, 72)
    gw_zl()
    backward(1, 72, 108)
    cross_z(0)
    backward(1, 108, 144)
    collect(1)
    core_start(1)
    cross_own(0)
    gw_back_zh()
    cross_start(1, 0)
    cross_start(1, 1)
    gw_back_x()
    cross_end(0)
    cross_z(1)
    gw_back_core()
    cross_own(1)
    gw_end()
    cross_end(1)
    for copy in sent.values():
        copy.wait_send()
    for copy in out:
        copy.wait()


def finish(act_in, gf_in, gw_in, act_out, gf_out, gw_out):
    act_out[...] = act_in[...]
    gf_out[...] = gf_in[...]
    gw_out[...] = gw_in[...]


def shards(features, weight, block_cols, edge_counts, cotangent):
    vmem = pl.BlockSpec(memory_space=pltpu.VMEM)
    smem = pl.BlockSpec(memory_space=pltpu.SMEM)
    anywhere = pl.BlockSpec(memory_space=pl.ANY)
    slab = pltpu.VMEM((48, TILE, TILE), BF16)

    def tiles(*lead, dtype=BF16):
        return pltpu.VMEM((*lead, TILE, TILE), dtype)

    def floats(*shape):
        return pltpu.VMEM(shape, F32)

    shapes = (
        jax.ShapeDtypeStruct((384, 256), BF16),
        jax.ShapeDtypeStruct((3, TILE, 256), BF16),
        jax.ShapeDtypeStruct((2, 4, 2, 16, 256), F32),
    )
    columns = jnp.transpose(block_cols, (2, 0, 1))
    results = pl.pallas_call(
        kernel,
        out_shape=shapes,
        in_specs=[smem, vmem] + [anywhere] * 4,
        out_specs=(anywhere,) * 3,
        scratch_shapes=[
            tiles(48, 3, dtype=jnp.int32),
            pltpu.VMEM((48, TILE, 3 * TILE), BF16),
            tiles(144),
            slab, slab, tiles(16, 3), tiles(16, 3),
            tiles(2, 4, 3, dtype=F32),
            tiles(2, 2, 2, 3),
            tiles(2, 2, 4, 3),
            tiles(2, 4, 3), tiles(2, 4, 3, dtype=F32), tiles(2, 4, 3),
            slab, slab,
            tiles(144),
            floats(TILE, TILE),
            tiles(4, 2, 2, 3), tiles(4, 2, 2, 3),
            tiles(2, 2, 4, 3), tiles(2, 2, 4, 3),
            tiles(2, 2, 3, dtype=F32),
            tiles(2, 2, 3, 3),
            tiles(2, 3, dtype=F32), tiles(2, 3), tiles(2, 3),
            floats(4, 4, 8, TILE), floats(4, 4, 8, TILE),
            floats(4, 8, TILE), floats(4, 8, TILE),
            pltpu.VMEM((256, 256), BF16),
            pltpu.VMEM((384, 256), BF16), pltpu.VMEM((384, 256), BF16),
            pltpu.VMEM((384, 256), BF16), pltpu.VMEM((384, 256), BF16),
            tiles(2, 3),
            floats(2, 4, 2, 16, 256),
            floats(4, 2, 16, 256), floats(4, 2, 16, 256),
            floats(4, 2, 16, 256), floats(2, 16, 256),
            floats(16, 256), floats(16, 256),
            floats(4, 16, 256), floats(16, 256),
            floats(4, 16, 256),
            floats(2, 4, 2, 16, 256),
            pltpu.VMEM((8, 256), jnp.int32), pltpu.VMEM((8, 256), F32),
            pltpu.SMEM((8, 256), jnp.int32), pltpu.SMEM((8, 256), F32),
            pltpu.SemaphoreType.DMA((16,)),
            pltpu.SemaphoreType.DMA((10,)),
            pltpu.SemaphoreType.DMA((MESSAGES,)),
            pltpu.SemaphoreType.DMA((MESSAGES,)),
        ],
        compiler_params=pltpu.CompilerParams(
            collective_id=0, has_side_effects=True, vmem_limit_bytes=62 << 20
        ),
        name="graph_layer",
    )(
        columns, columns, features[0].reshape(3, TILE, 256), weight, cotangent[0],
        edge_counts[0],
    )
    activated, grad_features, grad_weight = pl.pallas_call(
        finish,
        out_shape=shapes,
        in_specs=[vmem] * 3,
        out_specs=(vmem,) * 3,
        name="finish",
    )(*results)
    return (
        activated[None], grad_features.reshape(1, 384, 256), grad_weight.reshape(256, 256)
    )


def solution(mesh):
    placed = (
        P("rep", "row", None),
        P(),
        P("rep", "row", None),
        P("rep", "row", None, None, None),
        P("row", "rep", None),
    )
    return jax.shard_map(
        shards,
        mesh=mesh,
        in_specs=placed,
        out_specs=(P("row", "rep", None), P("rep", "row", None), P()),
        check_vma=False,
    )
```

time: 144 us -> 132 us (0.917)
  the two profiles are of different devices: /device:TPU:49 before, /device:TPU:1 now
where the time goes in v2:
time: 132 us
  Pallas kernels  131 us (99%)
    pallas_call x1, Pallas kernels, shards(): pl.pallas_call(kernel, out_shape=shapes, in_specs=[smem, vmem] + [anywher...  129 us

profile of v2, /device:TPU:1, one launch (start us, length us, event | category | flops | bytes accessed | tf_op | source)
XLA Modules:
  0.0 131.5 jit_solution(130924562021920638)
XLA Ops:
  0.6 128.9 %graph_layer.1 = (bf16[384,256]{1,0:T(8,128)(2,1)}, bf16[3,128,256]{2,1,0:T(8,128)(2,1)}, f32[2,4,2,16,256]{4,3,2,1,0:T(8,128)}) custom-call(s32[3,1,48]{2,1,0:T(1,128)} %bitcast.10, s32[3,1,48]{2,1,0:T(1,128)} %bitcast.11, bf16[3,128,256]{2,1,0:T(8,128)(2,1)} %bitcast.8, bf16[256,256]{1,0:T(8,128)(2,1)} %weight_hbm.1, bf16[384,256]{1,0:T(8,128)(2,1)} %bitcast.9, ...), custom_call_target="tpu_custom_call" | custom-call | tf_op jit(solution)/shard_map/graph_layer/pallas_call | solution.py:613
  129.5 2.0 %finish.1 = (bf16[384,256]{1,0:T(8,128)(2,1)}, bf16[3,128,256]{2,1,0:T(8,128)(2,1)}, f32[2,4,2,16,256]{4,3,2,1,0:T(8,128)}) custom-call(bf16[384,256]{1,0:T(8,128)(2,1)} %get-tuple-element.9.act_in, bf16[3,128,256]{2,1,0:T(8,128)(2,1)} %get-tuple-element.10.gf_in, f32[2,4,2,16,256]{4,3,2,1,0:T(8,128)} %get-tuple-element.11.gw_in), custom_call_target="tpu_custom_call" | custom-call | tf_op jit(solution)/shard_map/finish/pallas_call | solution.py:663

commit v3 on v2

--- a/solution.py
+++ b/solution.py
@@ -56,6 +56,13 @@
         )
         copy.start()
         sent[name] = copy
+
+    settled = [0]
+
+    def settle(upto):
+        for copy in list(sent.values())[settled[0] : upto]:
+            copy.wait_send()
+        settled[0] = upto
 
     def arrived(name):
         sent[name].wait_recv()
@@ -478,25 +485,24 @@
     a0, a1, b0, b1 = SPREAD_PARTS
     gather_z(0)
     gather_start(0)
-    convert(0, 5)
+    convert(0,10)
+    gather_near(0)
+    gather_start(1)
+    convert(10,16)
+    gather_far(0)
     gather_z(1)
-    gather_start(1)
-    convert(5, 10)
-    gather_near(0)
-    convert(10, 16)
-    gather_far(0)
     gather_near2(0)
     gather_near(1)
     degree_start()
-    gather_far(1)
+    gather_far2(0)
     gather_near2(1)
-    gather_far2(0)
     gather_end(0)
     reduce_start(s0)
     reduce_near(s0)
-    gather_far2(1)
+    gather_far(1)
     reduce_own(s0)
     degree_z()
+    gather_far2(1)
     reduce_relay(s0)
     gather_end(1)
     reduce_start(s1)
@@ -515,12 +521,13 @@
     sort_end()
     acc[...] = jnp.zeros_like(acc)
     reduce_z(s1)
+    reduce_z(s2)
+    before_dense = len(sent)
     dense_wait(s0)
     dense_wait(s1)
     dense(scale, 0, 1)
     spread_start(a0)
     spread_start(a1)
-    reduce_z(s2)
     spread_y(a0, 0)
     spread_y(a1, 0)
     for d in (1, 2, 3):
@@ -580,8 +587,7 @@
     cross_own(1)
     gw_end()
     cross_end(1)
-    for copy in sent.values():
-        copy.wait_send()
+    settle(len(sent))
     for copy in out:
         copy.wait()
 

time: 132 us -> 128 us (0.970)
  Pallas kernels: 131 us -> 127 us
    pallas_call x1, Pallas kernels: 129 us -> 125 us  [shards(): pl.pallas_call(kernel, out_shape=shapes, in_specs=[smem, vmem] + [anywher...]
where the time goes in v3:
time: 128 us
  Pallas kernels  127 us (99%)
    pallas_call x1, Pallas kernels, shards(): pl.pallas_call(kernel, out_shape=shapes, in_specs=[smem, vmem] + [anywher...  125 us

profile of v3, /device:TPU:1, one launch (start us, length us, event | category | flops | bytes accessed | tf_op | source)
XLA Modules:
  0.0 128.1 jit_solution(8270374742094249467)
XLA Ops:
  0.6 125.5 %graph_layer.1 = (bf16[384,256]{1,0:T(8,128)(2,1)}, bf16[3,128,256]{2,1,0:T(8,128)(2,1)}, f32[2,4,2,16,256]{4,3,2,1,0:T(8,128)}) custom-call(s32[3,1,48]{2,1,0:T(1,128)} %bitcast.10, s32[3,1,48]{2,1,0:T(1,128)} %bitcast.11, bf16[3,128,256]{2,1,0:T(8,128)(2,1)} %bitcast.8, bf16[256,256]{1,0:T(8,128)(2,1)} %weight_hbm.1, bf16[384,256]{1,0:T(8,128)(2,1)} %bitcast.9, ...), custom_call_target="tpu_custom_call" | custom-call | tf_op jit(solution)/shard_map/graph_layer/pallas_call | solution.py:619
  126.1 2.0 %finish.1 = (bf16[384,256]{1,0:T(8,128)(2,1)}, bf16[3,128,256]{2,1,0:T(8,128)(2,1)}, f32[2,4,2,16,256]{4,3,2,1,0:T(8,128)}) custom-call(bf16[384,256]{1,0:T(8,128)(2,1)} %get-tuple-element.9.act_in, bf16[3,128,256]{2,1,0:T(8,128)(2,1)} %get-tuple-element.10.gf_in, f32[2,4,2,16,256]{4,3,2,1,0:T(8,128)} %get-tuple-element.11.gw_in), custom_call_target="tpu_custom_call" | custom-call | tf_op jit(solution)/shard_map/finish/pallas_call | solution.py:669

commit v4 on v3

--- a/solution.py
+++ b/solution.py
@@ -337,10 +337,10 @@
 
     def spread_start(part):
         mine = chunk(part, own_rep)
+        send(("sp0", part), mine, mine, to_yp)
+        send(("sm0", part), mine, mine, to_ym)
         for d in (2, 1, 3):
             send(("sz%d" % d, part), mine, mine, to_z[d])
-        send(("sp0", part), mine, mine, to_yp)
-        send(("sm0", part), mine, mine, to_ym)
 
     def spread_z(part, d):
         arrived(("sz%d" % d, part))
@@ -502,8 +502,8 @@
     gather_far(1)
     reduce_own(s0)
     degree_z()
+    reduce_relay(s0)
     gather_far2(1)
-    reduce_relay(s0)
     gather_end(1)
     reduce_start(s1)
     reduce_near(s1)

time: 128 us -> 128 us (level)
  no operation moved by 1% of the time
where the time goes in v4:
time: 128 us
  Pallas kernels  127 us (99%)
    pallas_call x1, Pallas kernels, shards(): pl.pallas_call(kernel, out_shape=shapes, in_specs=[smem, vmem] + [anywher...  125 us

profile of v4, /device:TPU:1, one launch (start us, length us, event | category | flops | bytes accessed | tf_op | source)
XLA Modules:
  0.0 128.1 jit_solution(15628068139108341123)
XLA Ops:
  0.6 125.5 %graph_layer.1 = (bf16[384,256]{1,0:T(8,128)(2,1)}, bf16[3,128,256]{2,1,0:T(8,128)(2,1)}, f32[2,4,2,16,256]{4,3,2,1,0:T(8,128)}) custom-call(s32[3,1,48]{2,1,0:T(1,128)} %bitcast.10, s32[3,1,48]{2,1,0:T(1,128)} %bitcast.11, bf16[3,128,256]{2,1,0:T(8,128)(2,1)} %bitcast.8, bf16[256,256]{1,0:T(8,128)(2,1)} %weight_hbm.1, bf16[384,256]{1,0:T(8,128)(2,1)} %bitcast.9, ...), custom_call_target="tpu_custom_call" | custom-call | tf_op jit(solution)/shard_map/graph_layer/pallas_call | solution.py:619
  126.1 2.0 %finish.1 = (bf16[384,256]{1,0:T(8,128)(2,1)}, bf16[3,128,256]{2,1,0:T(8,128)(2,1)}, f32[2,4,2,16,256]{4,3,2,1,0:T(8,128)}) custom-call(bf16[384,256]{1,0:T(8,128)(2,1)} %get-tuple-element.9.act_in, bf16[3,128,256]{2,1,0:T(8,128)(2,1)} %get-tuple-element.10.gf_in, f32[2,4,2,16,256]{4,3,2,1,0:T(8,128)} %get-tuple-element.11.gw_in), custom_call_target="tpu_custom_call" | custom-call | tf_op jit(solution)/shard_map/finish/pallas_call | solution.py:669
